TPU v7x, 256 devices: a whole 4x4x8 slice. The times are simulated.
256 devices in a mesh: pipe: 16 (over y, z_lo), expert: 16 (over x, z_hi, core).
Axes of the slice: x: 4, y: 4, z: 8 (z_hi: 2, z_lo: 4; z = z_hi * 4 + z_lo), core: 2. Of those that a mesh axis runs over, the one named last changes fastest.
Arguments:
- entering: bfloat16 [2, 512, 2048], P(None, 'expert'), may hold values from -6 to 6
- first_gain: float32 [16, 2048], P('pipe'), may hold values from 0.1 to 1.9
- first_gate: bfloat16 [16, 16, 2048, 384], P('pipe', 'expert'), may hold values from -0.125 to 0.125
- first_up: bfloat16 [16, 16, 2048, 384], P('pipe', 'expert'), may hold values from -0.125 to 0.125
- first_down: bfloat16 [16, 16, 384, 2048], P('pipe', 'expert'), may hold values from -0.3125 to 0.3125
- first_route: int32 [16, 2, 512, 1], P('pipe', None, 'expert'), may hold values from 0 to 15; in each aligned block of 32 rows (0 to 31, 32 to 63, ..., all dimensions but the last counted through in order) at most 4 rows name the same one
- first_share: float32 [16, 2, 512], P('pipe', None, 'expert'), may hold values from 0.2 to 1
- saved_inputs: bfloat16 [16, 2, 512, 2048], P('pipe', None, 'expert'), may hold values from -6 to 6
- cotangent: bfloat16 [2, 512, 2048], P(None, 'expert'), may hold values from -6 to 6
- second_gain: float32 [16, 2048], P('pipe'), may hold values from 0.1 to 1.9
- second_gate: bfloat16 [16, 16, 2048, 384], P('pipe', 'expert'), may hold values from -0.125 to 0.125
- second_up: bfloat16 [16, 16, 2048, 384], P('pipe', 'expert'), may hold values from -0.125 to 0.125
- second_down: bfloat16 [16, 16, 384, 2048], P('pipe', 'expert'), may hold values from -0.3125 to 0.3125
- second_route: int32 [16, 2, 512, 1], P('pipe', None, 'expert'), may hold values from 0 to 15; in each aligned block of 32 rows (0 to 31, 32 to 63, ..., all dimensions but the last counted through in order) at most 4 rows name the same one
- second_share: float32 [16, 2, 512], P('pipe', None, 'expert'), may hold values from 0.2 to 1
Outputs:
- forward_states: bfloat16 [16, 2, 512, 2048], P('pipe', None, 'expert')
- input_grads: bfloat16 [16, 2, 512, 2048], P('pipe', None, 'expert')
Inputs may be any that keep to these rules, and one draw needn't show every extreme that they name: `first_route`: in each aligned block of 32 rows (the tokens of one device in one layer and micro-batch) no expert is named by more than 4 rows. `second_route`: in each aligned block of 32 rows (the tokens of one device in one layer and micro-batch) no expert is named by more than 4 rows.
All inputs are finite; a program needn't handle non-finite values.
Results may differ from a plain program's by a relative error of at most 0.035.
Values may be sent and summed in bfloat16 or wider, within the bound.
A program may use at most 64 MiB of HBM per device.

v0:
```python
import jax
import jax.numpy as jnp
from jax import lax
from jax.sharding import PartitionSpec as P

TOP = 1


EPSILON = 1e-06


def from_behind(array, axis, by):
    peers = lax.axis_size(axis)
    pairs = [(i, i + by) for i in range(peers) if 0 <= i + by < peers]
    return lax.ppermute(array, axis, pairs)


def rms_scaled(values, gain_vector):
    squares = jnp.mean(values * values, axis=-1, keepdims=True)
    return values * lax.rsqrt(squares + EPSILON) * gain_vector


def expert_forward(expert_rows, gate_w, up_w, down_w):
    pre_gate = jnp.dot(expert_rows, gate_w, preferred_element_type=jnp.float32)
    pre_up = jnp.dot(expert_rows, up_w, preferred_element_type=jnp.float32)
    hidden = (jax.nn.silu(pre_gate) * pre_up).astype(jnp.bfloat16)
    return jnp.dot(hidden, down_w, preferred_element_type=jnp.float32).astype(jnp.bfloat16)


def expert_backward(expert_rows, sent_rows, gate_w, up_w, down_w):
    back_gate = jnp.dot(expert_rows, gate_w, preferred_element_type=jnp.float32)
    back_up = jnp.dot(expert_rows, up_w, preferred_element_type=jnp.float32)
    d_hidden = lax.dot_general(
        sent_rows, down_w, (((1,), (1,)), ((), ())), preferred_element_type=jnp.float32
    )
    sigmoid_gate = jax.nn.sigmoid(back_gate)
    d_gate = (d_hidden * back_up * sigmoid_gate * (1.0 + back_gate * (1.0 - sigmoid_gate))).astype(
        jnp.bfloat16
    )
    d_up = (d_hidden * back_gate * sigmoid_gate).astype(jnp.bfloat16)
    first_term = lax.dot_general(
        d_gate, gate_w, (((1,), (1,)), ((), ())), preferred_element_type=jnp.float32
    )
    second_term = lax.dot_general(
        d_up, up_w, (((1,), (1,)), ((), ())), preferred_element_type=jnp.float32
    )
    return (first_term + second_term).astype(jnp.bfloat16)


def local(
    entering,
    first_gain,
    first_gate,
    first_up,
    first_down,
    first_route,
    first_share,
    saved_inputs,
    cotangent,
    second_gain,
    second_gate,
    second_up,
    second_down,
    second_route,
    second_share,
):
    sections = lax.axis_size("pipe")
    group_size = lax.axis_size("expert")
    micro_count = entering.shape[0]
    token_count = entering.shape[1]
    feature_width = entering.shape[2]
    capacity = 2 * token_count * TOP // group_size
    position = lax.axis_index("pipe")
    turns = micro_count + sections - 1

    def dispatch_table(route_ids):
        member = (route_ids[:, None] == jnp.arange(group_size, dtype=jnp.int32)[None, :]).astype(
            jnp.int32
        )
        before = jnp.cumsum(member, axis=0) - member
        slots = jnp.sum(member * before, axis=-1)
        target = route_ids * capacity + slots
        return (
            target[:, None] == jnp.arange(group_size * capacity, dtype=jnp.int32)[None, :]
        ).astype(jnp.bfloat16)

    def to_experts(table, values):
        placed = jnp.dot(table.T, values, preferred_element_type=jnp.float32).astype(jnp.bfloat16)
        return placed.reshape(group_size, capacity, feature_width)

    def from_experts(table, returned):
        return jnp.dot(
            table,
            returned.reshape(group_size * capacity, feature_width),
            preferred_element_type=jnp.float32,
        )

    def forward_rows(received):
        flattened = received.reshape(-1, feature_width)
        result = expert_forward(flattened, first_gate[0, 0], first_up[0, 0], first_down[0, 0])
        return result.reshape(received.shape)

    def backward_rows(received_rows, received_sent):
        flattened = received_rows.reshape(-1, feature_width)
        flat_sent = received_sent.reshape(-1, feature_width)
        result = expert_backward(
            flattened, flat_sent, second_gate[0, 0], second_up[0, 0], second_down[0, 0]
        )
        return result.reshape(received_rows.shape)

    def layer_work(input_forward, upstream, chosen):
        route_forward = lax.dynamic_index_in_dim(first_route[0], chosen, 0, keepdims=False)[:, 0]
        share_forward = lax.dynamic_index_in_dim(first_share[0], chosen, 0, keepdims=False)
        table_forward = dispatch_table(route_forward)
        normed_forward = rms_scaled(input_forward.astype(jnp.float32), first_gain[0]).astype(
            jnp.bfloat16
        )
        send_forward = to_experts(table_forward, normed_forward)
        saved_rows = lax.dynamic_index_in_dim(saved_inputs[0], chosen, 0, keepdims=False)
        route_backward = lax.dynamic_index_in_dim(second_route[0], chosen, 0, keepdims=False)[:, 0]
        share_backward = lax.dynamic_index_in_dim(second_share[0], chosen, 0, keepdims=False)
        table_backward = dispatch_table(route_backward)
        normed_backward, pullback = jax.vjp(
            lambda values: rms_scaled(values, second_gain[0]), saved_rows.astype(jnp.float32)
        )
        normed_backward = normed_backward.astype(jnp.bfloat16)
        sent_rows = (share_backward[:, None] * upstream.astype(jnp.float32)).astype(jnp.bfloat16)
        send_saved = to_experts(table_backward, normed_backward)
        send_grads = to_experts(table_backward, sent_rows)
        back_forward = lax.all_to_all(
            forward_rows(
                lax.all_to_all(send_forward, "expert", split_axis=0, concat_axis=0, tiled=True)
            ),
            "expert",
            split_axis=0,
            concat_axis=0,
            tiled=True,
        )
        rows_backward = lax.all_to_all(
            send_saved, "expert", split_axis=0, concat_axis=0, tiled=True
        )
        rows_sent = lax.all_to_all(send_grads, "expert", split_axis=0, concat_axis=0, tiled=True)
        back_backward = lax.all_to_all(
            backward_rows(rows_backward, rows_sent),
            "expert",
            split_axis=0,
            concat_axis=0,
            tiled=True,
        )
        output_forward = (
            input_forward.astype(jnp.float32)
            + share_forward[:, None] * from_experts(table_forward, back_forward)
        ).astype(jnp.bfloat16)
        output_backward = (
            upstream.astype(jnp.float32) + pullback(from_experts(table_backward, back_backward))[0]
        ).astype(jnp.bfloat16)
        return (output_forward, output_backward)

    def turn_body(turn_index, loop_state):
        carry_forward, carry_backward, states_forward, states_backward = loop_state
        micro_index = turn_index - position
        active = jnp.logical_and(micro_index >= 0, micro_index < micro_count)
        chosen = jnp.clip(micro_index, 0, micro_count - 1)
        entry_index = jnp.minimum(turn_index, micro_count - 1)
        fresh_input = lax.dynamic_index_in_dim(entering, entry_index, 0, keepdims=False)
        fresh_grad = lax.dynamic_index_in_dim(cotangent, entry_index, 0, keepdims=False)
        input_forward = jnp.where(position == 0, fresh_input, carry_forward)
        upstream = jnp.where(position == 0, fresh_grad, carry_backward)
        output_forward, output_backward = layer_work(input_forward, upstream, chosen)
        states_forward = jnp.where(
            active,
            lax.dynamic_update_index_in_dim(states_forward, output_forward, chosen, 0),
            states_forward,
        )
        states_backward = jnp.where(
            active,
            lax.dynamic_update_index_in_dim(states_backward, output_backward, chosen, 0),
            states_backward,
        )
        next_forward, next_backward = from_behind((output_forward, output_backward), "pipe", 1)
        return (next_forward, next_backward, states_forward, states_backward)

    zero_rows = jnp.zeros((token_count, feature_width), jnp.bfloat16)
    zero_states = jnp.zeros((micro_count, token_count, feature_width), jnp.bfloat16)
    final_state = lax.fori_loop(
        0, turns, turn_body, (zero_rows, zero_rows, zero_states, zero_states)
    )
    return (final_state[2][None], final_state[3][None])


def solution(mesh):
    return jax.shard_map(
        local,
        mesh=mesh,
        in_specs=(
            P(None, "expert", None),
            P("pipe", None),
            P("pipe", "expert", None, None),
            P("pipe", "expert", None, None),
            P("pipe", "expert", None, None),
            P("pipe", None, "expert", None),
            P("pipe", None, "expert"),
            P("pipe", None, "expert", None),
            P(None, "expert", None),
            P("pipe", None),
            P("pipe", "expert", None, None),
            P("pipe", "expert", None, None),
            P("pipe", "expert", None, None),
            P("pipe", None, "expert", None),
            P("pipe", None, "expert"),
        ),
        out_specs=(P("pipe", None, "expert", None), P("pipe", None, "expert", None)),
        check_vma=False,
    )
```

profile of v0, /device:TPU:40, one launch (start us, length us, event | category | flops | bytes accessed | tf_op | source)
XLA Modules:
  0.0 1699.5 jit_solution(5868538437424042977)
XLA Ops:
  2.8 1696.7 %while.20 = (s32[]{:T(128)}, bf16[32,2048]{1,0:T(8,128)(2,1)}, bf16[32,2048]{1,0:T(8,128)(2,1)S(1)}, bf16[2,32,2048]{2,1,0:T(8,128)(2,1)}, bf16[2,32,2048]{2,1,0...) while((s32[]{:T(128)}, bf16[32,2048]{1,0:T(8,128)(2,1)}, ...), condition=%wide.region_8.9_spmd, body=%wide.region_0.8_spmd.sunk | while | flops 851116352 | bytes 66541944 | solution.py:185
  7.5 10.1 all-to-all-start
  19.4 13.0 all-to-all-done
  41.4 8.2 all-to-all-done.2
  92.8 7.9 all-to-all-done.4
  118.3 13.0 all-to-all-done
  140.2 7.5 all-to-all-done.2
  164.0 5.7 all-to-all-start.1
  193.2 5.6 all-to-all-done.4
  217.3 13.0 all-to-all-done
  239.3 8.8 all-to-all-done.2
  264.4 5.6 all-to-all-start.1
  291.1 10.6 all-to-all-done.4
  319.3 10.4 all-to-all-done
  338.6 7.3 all-to-all-done.2
  362.0 5.7 all-to-all-start.1
  415.5 13.0 all-to-all-done
  437.4 8.8 all-to-all-done.2
  489.3 10.7 all-to-all-done.4
  517.5 10.3 all-to-all-done
  536.8 7.3 all-to-all-done.2
  560.2 5.7 all-to-all-start.1
  613.7 13.0 all-to-all-done
  635.6 8.8 all-to-all-done.2
  687.5 8.1 all-to-all-done.4
  713.2 13.0 all-to-all-done
  735.1 7.6 all-to-all-done.2
  758.9 5.6 all-to-all-start.1
  788.2 5.6 all-to-all-done.4
  812.7 13.0 all-to-all-done
  834.6 9.0 all-to-all-done.2
  859.9 5.6 all-to-all-start.1
  886.3 8.4 all-to-all-done.4
  912.3 12.6 all-to-all-done
  933.8 7.3 all-to-all-done.2
  957.4 5.7 all-to-all-start.1
  992.9 6.4 collective-permute-start.1
  1012.2 13.0 all-to-all-done
  1034.2 9.0 all-to-all-done.2
  1085.8 11.4 all-to-all-done.4
  1114.7 10.2 all-to-all-done
  1133.9 7.2 all-to-all-done.2
  1157.3 5.7 all-to-all-start.1
  1186.7 8.2 all-to-all-done.4
  1212.5 12.8 all-to-all-done
  1234.2 7.3 all-to-all-done.2
  1257.7 5.7 all-to-all-start.1
  1284.5 10.9 all-to-all-done.4
  1313.0 10.2 all-to-all-done
  1332.1 7.2 all-to-all-done.2
  1355.5 5.7 all-to-all-start.1
  1384.9 8.2 all-to-all-done.4
  1410.7 12.8 all-to-all-done
  1432.4 7.3 all-to-all-done.2
  1456.0 5.7 all-to-all-start.1
  1482.8 10.9 all-to-all-done.4
  1511.2 10.2 all-to-all-done
  1530.4 7.2 all-to-all-done.2
  1553.8 5.7 all-to-all-start.1
  1583.2 8.1 all-to-all-done.4
  1608.8 12.9 all-to-all-done
  1630.7 7.3 all-to-all-done.2
  1654.2 5.7 all-to-all-start.1
  1681.0 10.9 all-to-all-done.4
  (1624 shorter events, 1135.7 us)
Async XLA Ops:
  7.5 24.9 %all-to-all-start = ((bf16[16,4,2048]{2,1,0:T(4,128)(2,1)}), bf16[16,4,2048]{2,1,0:T(4,128)(2,1)S(1)}, u32[]{:S(2)}, u32[]{:S(2)}) async-start(bf16[16,4,2048]{2,1,0:T(4,128)(2,1)} %reshape.175), calls=%async_computation | async-start | bytes 524288 | tf_op jit(solution)/shard_map/while/body/eval_jaxpr/all_to_all | solution.py:132
  32.4 17.2 %all-to-all-start.2 = ((bf16[16,4,2048]{2,1,0:T(4,128)(2,1)}), bf16[16,4,2048]{2,1,0:T(4,128)(2,1)}, u32[]{:S(2)}, u32[]{:S(2)}) async-start(bf16[16,4,2048]{2,1,0:T(4,128)(2,1)} %reshape.179), calls=%async_computation.2 | async-start | bytes 524288 | tf_op jit(solution)/shard_map/while/body/eval_jaxpr/all_to_all | solution.py:142
  49.6 16.3 all-to-all-start.3
  65.9 17.7 %all-to-all-start.1 = ((bf16[16,4,2048]{2,1,0:T(4,128)(2,1)}), bf16[16,4,2048]{2,1,0:T(4,128)(2,1)}, u32[]{:S(2)}, u32[]{:S(2)}) async-start(bf16[16,4,2048]{2,1,0:T(4,128)(2,1)} %reshape.177), calls=%async_computation.1 | async-start | bytes 524288 | tf_op jit(solution)/shard_map/while/body/eval_jaxpr/all_to_all | solution.py:130
  83.6 17.2 %all-to-all-start.4 = ((bf16[16,4,2048]{2,1,0:T(4,128)(2,1)}), bf16[16,4,2048]{2,1,0:T(4,128)(2,1)S(1)}, u32[]{:S(2)}, u32[]{:S(2)}) async-start(bf16[16,4,2048]{2,1,0:T(4,128)(2,1)} %reshape.183), calls=%async_computation.4 | async-start | bytes 524288 | tf_op jit(solution)/shard_map/while/body/eval_jaxpr/all_to_all | solution.py:143
  113.0 18.3 %all-to-all-start = ((bf16[16,4,2048]{2,1,0:T(4,128)(2,1)}), bf16[16,4,2048]{2,1,0:T(4,128)(2,1)S(1)}, u32[]{:S(2)}, u32[]{:S(2)}) async-start(bf16[16,4,2048]{2,1,0:T(4,128)(2,1)} %reshape.175), calls=%async_computation | async-start | bytes 524288 | tf_op jit(solution)/shard_map/while/body/eval_jaxpr/all_to_all | solution.py:132
  131.3 16.5 all-to-all-start.2
  164.0 17.7 %all-to-all-start.1 = ((bf16[16,4,2048]{2,1,0:T(4,128)(2,1)}), bf16[16,4,2048]{2,1,0:T(4,128)(2,1)}, u32[]{:S(2)}, u32[]{:S(2)}) async-start(bf16[16,4,2048]{2,1,0:T(4,128)(2,1)} %reshape.177), calls=%async_computation.1 | async-start | bytes 524288 | tf_op jit(solution)/shard_map/while/body/eval_jaxpr/all_to_all | solution.py:130
  181.7 17.2 %all-to-all-start.4 = ((bf16[16,4,2048]{2,1,0:T(4,128)(2,1)}), bf16[16,4,2048]{2,1,0:T(4,128)(2,1)S(1)}, u32[]{:S(2)}, u32[]{:S(2)}) async-start(bf16[16,4,2048]{2,1,0:T(4,128)(2,1)} %reshape.183), calls=%async_computation.4 | async-start | bytes 524288 | tf_op jit(solution)/shard_map/while/body/eval_jaxpr/all_to_all | solution.py:143
  188.1 16.7 collective-permute-start
  212.1 18.3 %all-to-all-start = ((bf16[16,4,2048]{2,1,0:T(4,128)(2,1)}), bf16[16,4,2048]{2,1,0:T(4,128)(2,1)S(1)}, u32[]{:S(2)}, u32[]{:S(2)}) async-start(bf16[16,4,2048]{2,1,0:T(4,128)(2,1)} %reshape.175), calls=%async_computation | async-start | bytes 524288 | tf_op jit(solution)/shard_map/while/body/eval_jaxpr/all_to_all | solution.py:132
  230.3 17.8 %all-to-all-start.2 = ((bf16[16,4,2048]{2,1,0:T(4,128)(2,1)}), bf16[16,4,2048]{2,1,0:T(4,128)(2,1)}, u32[]{:S(2)}, u32[]{:S(2)}) async-start(bf16[16,4,2048]{2,1,0:T(4,128)(2,1)} %reshape.179), calls=%async_computation.2 | async-start | bytes 524288 | tf_op jit(solution)/shard_map/while/body/eval_jaxpr/all_to_all | solution.py:142
  248.1 16.3 all-to-all-start.3
  264.4 17.7 %all-to-all-start.1 = ((bf16[16,4,2048]{2,1,0:T(4,128)(2,1)}), bf16[16,4,2048]{2,1,0:T(4,128)(2,1)}, u32[]{:S(2)}, u32[]{:S(2)}) async-start(bf16[16,4,2048]{2,1,0:T(4,128)(2,1)} %reshape.177), calls=%async_computation.1 | async-start | bytes 524288 | tf_op jit(solution)/shard_map/while/body/eval_jaxpr/all_to_all | solution.py:130
  282.1 19.7 %all-to-all-start.4 = ((bf16[16,4,2048]{2,1,0:T(4,128)(2,1)}), bf16[16,4,2048]{2,1,0:T(4,128)(2,1)S(1)}, u32[]{:S(2)}, u32[]{:S(2)}) async-start(bf16[16,4,2048]{2,1,0:T(4,128)(2,1)} %reshape.183), calls=%async_computation.4 | async-start | bytes 524288 | tf_op jit(solution)/shard_map/while/body/eval_jaxpr/all_to_all | solution.py:143
  362.0 17.7 %all-to-all-start.1 = ((bf16[16,4,2048]{2,1,0:T(4,128)(2,1)}), bf16[16,4,2048]{2,1,0:T(4,128)(2,1)}, u32[]{:S(2)}, u32[]{:S(2)}) async-start(bf16[16,4,2048]{2,1,0:T(4,128)(2,1)} %reshape.177), calls=%async_computation.1 | async-start | bytes 524288 | tf_op jit(solution)/shard_map/while/body/eval_jaxpr/all_to_all | solution.py:130
  379.8 17.2 %all-to-all-start.4 = ((bf16[16,4,2048]{2,1,0:T(4,128)(2,1)}), bf16[16,4,2048]{2,1,0:T(4,128)(2,1)S(1)}, u32[]{:S(2)}, u32[]{:S(2)}) async-start(bf16[16,4,2048]{2,1,0:T(4,128)(2,1)} %reshape.183), calls=%async_computation.4 | async-start | bytes 524288 | tf_op jit(solution)/shard_map/while/body/eval_jaxpr/all_to_all | solution.py:143
  386.2 16.8 collective-permute-start
  410.2 18.3 %all-to-all-start = ((bf16[16,4,2048]{2,1,0:T(4,128)(2,1)}), bf16[16,4,2048]{2,1,0:T(4,128)(2,1)S(1)}, u32[]{:S(2)}, u32[]{:S(2)}) async-start(bf16[16,4,2048]{2,1,0:T(4,128)(2,1)} %reshape.175), calls=%async_computation | async-start | bytes 524288 | tf_op jit(solution)/shard_map/while/body/eval_jaxpr/all_to_all | solution.py:132
  428.5 17.8 %all-to-all-start.2 = ((bf16[16,4,2048]{2,1,0:T(4,128)(2,1)}), bf16[16,4,2048]{2,1,0:T(4,128)(2,1)}, u32[]{:S(2)}, u32[]{:S(2)}) async-start(bf16[16,4,2048]{2,1,0:T(4,128)(2,1)} %reshape.179), calls=%async_computation.2 | async-start | bytes 524288 | tf_op jit(solution)/shard_map/while/body/eval_jaxpr/all_to_all | solution.py:142
  462.5 17.7 %all-to-all-start.1 = ((bf16[16,4,2048]{2,1,0:T(4,128)(2,1)}), bf16[16,4,2048]{2,1,0:T(4,128)(2,1)}, u32[]{:S(2)}, u32[]{:S(2)}) async-start(bf16[16,4,2048]{2,1,0:T(4,128)(2,1)} %reshape.177), calls=%async_computation.1 | async-start | bytes 524288 | tf_op jit(solution)/shard_map/while/body/eval_jaxpr/all_to_all | solution.py:130
  480.2 19.7 %all-to-all-start.4 = ((bf16[16,4,2048]{2,1,0:T(4,128)(2,1)}), bf16[16,4,2048]{2,1,0:T(4,128)(2,1)S(1)}, u32[]{:S(2)}, u32[]{:S(2)}) async-start(bf16[16,4,2048]{2,1,0:T(4,128)(2,1)} %reshape.183), calls=%async_computation.4 | async-start | bytes 524288 | tf_op jit(solution)/shard_map/while/body/eval_jaxpr/all_to_all | solution.py:143
  560.2 17.7 %all-to-all-start.1 = ((bf16[16,4,2048]{2,1,0:T(4,128)(2,1)}), bf16[16,4,2048]{2,1,0:T(4,128)(2,1)}, u32[]{:S(2)}, u32[]{:S(2)}) async-start(bf16[16,4,2048]{2,1,0:T(4,128)(2,1)} %reshape.177), calls=%async_computation.1 | async-start | bytes 524288 | tf_op jit(solution)/shard_map/while/body/eval_jaxpr/all_to_all | solution.py:130
  577.9 17.2 %all-to-all-start.4 = ((bf16[16,4,2048]{2,1,0:T(4,128)(2,1)}), bf16[16,4,2048]{2,1,0:T(4,128)(2,1)S(1)}, u32[]{:S(2)}, u32[]{:S(2)}) async-start(bf16[16,4,2048]{2,1,0:T(4,128)(2,1)} %reshape.183), calls=%async_computation.4 | async-start | bytes 524288 | tf_op jit(solution)/shard_map/while/body/eval_jaxpr/all_to_all | solution.py:143
  584.3 16.8 collective-permute-start
  608.4 18.3 %all-to-all-start = ((bf16[16,4,2048]{2,1,0:T(4,128)(2,1)}), bf16[16,4,2048]{2,1,0:T(4,128)(2,1)S(1)}, u32[]{:S(2)}, u32[]{:S(2)}) async-start(bf16[16,4,2048]{2,1,0:T(4,128)(2,1)} %reshape.175), calls=%async_computation | async-start | bytes 524288 | tf_op jit(solution)/shard_map/while/body/eval_jaxpr/all_to_all | solution.py:132
  626.7 17.8 %all-to-all-start.2 = ((bf16[16,4,2048]{2,1,0:T(4,128)(2,1)}), bf16[16,4,2048]{2,1,0:T(4,128)(2,1)}, u32[]{:S(2)}, u32[]{:S(2)}) async-start(bf16[16,4,2048]{2,1,0:T(4,128)(2,1)} %reshape.179), calls=%async_computation.2 | async-start | bytes 524288 | tf_op jit(solution)/shard_map/while/body/eval_jaxpr/all_to_all | solution.py:142
  660.7 17.7 %all-to-all-start.1 = ((bf16[16,4,2048]{2,1,0:T(4,128)(2,1)}), bf16[16,4,2048]{2,1,0:T(4,128)(2,1)}, u32[]{:S(2)}, u32[]{:S(2)}) async-start(bf16[16,4,2048]{2,1,0:T(4,128)(2,1)} %reshape.177), calls=%async_computation.1 | async-start | bytes 524288 | tf_op jit(solution)/shard_map/while/body/eval_jaxpr/all_to_all | solution.py:130
  678.4 17.2 %all-to-all-start.4 = ((bf16[16,4,2048]{2,1,0:T(4,128)(2,1)}), bf16[16,4,2048]{2,1,0:T(4,128)(2,1)S(1)}, u32[]{:S(2)}, u32[]{:S(2)}) async-start(bf16[16,4,2048]{2,1,0:T(4,128)(2,1)} %reshape.183), calls=%async_computation.4 | async-start | bytes 524288 | tf_op jit(solution)/shard_map/while/body/eval_jaxpr/all_to_all | solution.py:143
  707.9 18.3 %all-to-all-start = ((bf16[16,4,2048]{2,1,0:T(4,128)(2,1)}), bf16[16,4,2048]{2,1,0:T(4,128)(2,1)S(1)}, u32[]{:S(2)}, u32[]{:S(2)}) async-start(bf16[16,4,2048]{2,1,0:T(4,128)(2,1)} %reshape.175), calls=%async_computation | async-start | bytes 524288 | tf_op jit(solution)/shard_map/while/body/eval_jaxpr/all_to_all | solution.py:132
  726.2 16.5 all-to-all-start.2
  758.9 17.7 %all-to-all-start.1 = ((bf16[16,4,2048]{2,1,0:T(4,128)(2,1)}), bf16[16,4,2048]{2,1,0:T(4,128)(2,1)}, u32[]{:S(2)}, u32[]{:S(2)}) async-start(bf16[16,4,2048]{2,1,0:T(4,128)(2,1)} %reshape.177), calls=%async_computation.1 | async-start | bytes 524288 | tf_op jit(solution)/shard_map/while/body/eval_jaxpr/all_to_all | solution.py:130
  776.6 17.2 %all-to-all-start.4 = ((bf16[16,4,2048]{2,1,0:T(4,128)(2,1)}), bf16[16,4,2048]{2,1,0:T(4,128)(2,1)S(1)}, u32[]{:S(2)}, u32[]{:S(2)}) async-start(bf16[16,4,2048]{2,1,0:T(4,128)(2,1)} %reshape.183), calls=%async_computation.4 | async-start | bytes 524288 | tf_op jit(solution)/shard_map/while/body/eval_jaxpr/all_to_all | solution.py:143
  783.0 17.0 collective-permute-start
  807.4 18.3 %all-to-all-start = ((bf16[16,4,2048]{2,1,0:T(4,128)(2,1)}), bf16[16,4,2048]{2,1,0:T(4,128)(2,1)S(1)}, u32[]{:S(2)}, u32[]{:S(2)}) async-start(bf16[16,4,2048]{2,1,0:T(4,128)(2,1)} %reshape.175), calls=%async_computation | async-start | bytes 524288 | tf_op jit(solution)/shard_map/while/body/eval_jaxpr/all_to_all | solution.py:132
  825.7 17.9 %all-to-all-start.2 = ((bf16[16,4,2048]{2,1,0:T(4,128)(2,1)}), bf16[16,4,2048]{2,1,0:T(4,128)(2,1)}, u32[]{:S(2)}, u32[]{:S(2)}) async-start(bf16[16,4,2048]{2,1,0:T(4,128)(2,1)} %reshape.179), calls=%async_computation.2 | async-start | bytes 524288 | tf_op jit(solution)/shard_map/while/body/eval_jaxpr/all_to_all | solution.py:142
  859.9 17.7 %all-to-all-start.1 = ((bf16[16,4,2048]{2,1,0:T(4,128)(2,1)}), bf16[16,4,2048]{2,1,0:T(4,128)(2,1)}, u32[]{:S(2)}, u32[]{:S(2)}) async-start(bf16[16,4,2048]{2,1,0:T(4,128)(2,1)} %reshape.177), calls=%async_computation.1 | async-start | bytes 524288 | tf_op jit(solution)/shard_map/while/body/eval_jaxpr/all_to_all | solution.py:130
  877.6 17.2 %all-to-all-start.4 = ((bf16[16,4,2048]{2,1,0:T(4,128)(2,1)}), bf16[16,4,2048]{2,1,0:T(4,128)(2,1)S(1)}, u32[]{:S(2)}, u32[]{:S(2)}) async-start(bf16[16,4,2048]{2,1,0:T(4,128)(2,1)} %reshape.183), calls=%async_computation.4 | async-start | bytes 524288 | tf_op jit(solution)/shard_map/while/body/eval_jaxpr/all_to_all | solution.py:143
  907.1 17.8 %all-to-all-start = ((bf16[16,4,2048]{2,1,0:T(4,128)(2,1)}), bf16[16,4,2048]{2,1,0:T(4,128)(2,1)S(1)}, u32[]{:S(2)}, u32[]{:S(2)}) async-start(bf16[16,4,2048]{2,1,0:T(4,128)(2,1)} %reshape.175), calls=%async_computation | async-start | bytes 524288 | tf_op jit(solution)/shard_map/while/body/eval_jaxpr/all_to_all | solution.py:132
  957.4 17.7 %all-to-all-start.1 = ((bf16[16,4,2048]{2,1,0:T(4,128)(2,1)}), bf16[16,4,2048]{2,1,0:T(4,128)(2,1)}, u32[]{:S(2)}, u32[]{:S(2)}) async-start(bf16[16,4,2048]{2,1,0:T(4,128)(2,1)} %reshape.177), calls=%async_computation.1 | async-start | bytes 524288 | tf_op jit(solution)/shard_map/while/body/eval_jaxpr/all_to_all | solution.py:130
  975.1 17.2 %all-to-all-start.4 = ((bf16[16,4,2048]{2,1,0:T(4,128)(2,1)}), bf16[16,4,2048]{2,1,0:T(4,128)(2,1)S(1)}, u32[]{:S(2)}, u32[]{:S(2)}) async-start(bf16[16,4,2048]{2,1,0:T(4,128)(2,1)} %reshape.183), calls=%async_computation.4 | async-start | bytes 524288 | tf_op jit(solution)/shard_map/while/body/eval_jaxpr/all_to_all | solution.py:143
  981.5 17.9 %collective-permute-start = (bf16[32,2048]{1,0:T(8,128)(2,1)S(1)}, bf16[32,2048]{1,0:T(8,128)(2,1)}, u32[]{:S(2)}, u32[]{:S(2)}) collective-permute-start(bf16[32,2048]{1,0:T(8,128)(2,1)S(1)} %get-tuple-element.623), channel_id=1, source_target_pairs={{0,16},{16,32},{32,48},{48,64},{64,80},{80,96},{96,112},{112,128},... | collective-permute-start | bytes 393224 | tf_op jit(solution)/shard_map/while/body/eval_jaxpr/ppermute | solution.py:15
  1007.0 18.3 %all-to-all-start = ((bf16[16,4,2048]{2,1,0:T(4,128)(2,1)}), bf16[16,4,2048]{2,1,0:T(4,128)(2,1)S(1)}, u32[]{:S(2)}, u32[]{:S(2)}) async-start(bf16[16,4,2048]{2,1,0:T(4,128)(2,1)} %reshape.175), calls=%async_computation | async-start | bytes 524288 | tf_op jit(solution)/shard_map/while/body/eval_jaxpr/all_to_all | solution.py:132
  1025.3 17.9 %all-to-all-start.2 = ((bf16[16,4,2048]{2,1,0:T(4,128)(2,1)}), bf16[16,4,2048]{2,1,0:T(4,128)(2,1)}, u32[]{:S(2)}, u32[]{:S(2)}) async-start(bf16[16,4,2048]{2,1,0:T(4,128)(2,1)} %reshape.179), calls=%async_computation.2 | async-start | bytes 524288 | tf_op jit(solution)/shard_map/while/body/eval_jaxpr/all_to_all | solution.py:142
  1059.4 17.7 %all-to-all-start.1 = ((bf16[16,4,2048]{2,1,0:T(4,128)(2,1)}), bf16[16,4,2048]{2,1,0:T(4,128)(2,1)}, u32[]{:S(2)}, u32[]{:S(2)}) async-start(bf16[16,4,2048]{2,1,0:T(4,128)(2,1)} %reshape.177), calls=%async_computation.1 | async-start | bytes 524288 | tf_op jit(solution)/shard_map/while/body/eval_jaxpr/all_to_all | solution.py:130
  1077.2 20.0 %all-to-all-start.4 = ((bf16[16,4,2048]{2,1,0:T(4,128)(2,1)}), bf16[16,4,2048]{2,1,0:T(4,128)(2,1)S(1)}, u32[]{:S(2)}, u32[]{:S(2)}) async-start(bf16[16,4,2048]{2,1,0:T(4,128)(2,1)} %reshape.183), calls=%async_computation.4 | async-start | bytes 524288 | tf_op jit(solution)/shard_map/while/body/eval_jaxpr/all_to_all | solution.py:143
  1157.3 17.7 %all-to-all-start.1 = ((bf16[16,4,2048]{2,1,0:T(4,128)(2,1)}), bf16[16,4,2048]{2,1,0:T(4,128)(2,1)}, u32[]{:S(2)}, u32[]{:S(2)}) async-start(bf16[16,4,2048]{2,1,0:T(4,128)(2,1)} %reshape.177), calls=%async_computation.1 | async-start | bytes 524288 | tf_op jit(solution)/shard_map/while/body/eval_jaxpr/all_to_all | solution.py:130
  1175.0 20.0 %all-to-all-start.4 = ((bf16[16,4,2048]{2,1,0:T(4,128)(2,1)}), bf16[16,4,2048]{2,1,0:T(4,128)(2,1)S(1)}, u32[]{:S(2)}, u32[]{:S(2)}) async-start(bf16[16,4,2048]{2,1,0:T(4,128)(2,1)} %reshape.183), calls=%async_computation.4 | async-start | bytes 524288 | tf_op jit(solution)/shard_map/while/body/eval_jaxpr/all_to_all | solution.py:143
  1181.4 16.8 collective-permute-start
  1207.2 18.0 %all-to-all-start = ((bf16[16,4,2048]{2,1,0:T(4,128)(2,1)}), bf16[16,4,2048]{2,1,0:T(4,128)(2,1)S(1)}, u32[]{:S(2)}, u32[]{:S(2)}) async-start(bf16[16,4,2048]{2,1,0:T(4,128)(2,1)} %reshape.175), calls=%async_computation | async-start | bytes 524288 | tf_op jit(solution)/shard_map/while/body/eval_jaxpr/all_to_all | solution.py:132
  1257.7 17.7 %all-to-all-start.1 = ((bf16[16,4,2048]{2,1,0:T(4,128)(2,1)}), bf16[16,4,2048]{2,1,0:T(4,128)(2,1)}, u32[]{:S(2)}, u32[]{:S(2)}) async-start(bf16[16,4,2048]{2,1,0:T(4,128)(2,1)} %reshape.177), calls=%async_computation.1 | async-start | bytes 524288 | tf_op jit(solution)/shard_map/while/body/eval_jaxpr/all_to_all | solution.py:130
  1275.4 20.0 %all-to-all-start.4 = ((bf16[16,4,2048]{2,1,0:T(4,128)(2,1)}), bf16[16,4,2048]{2,1,0:T(4,128)(2,1)S(1)}, u32[]{:S(2)}, u32[]{:S(2)}) async-start(bf16[16,4,2048]{2,1,0:T(4,128)(2,1)} %reshape.183), calls=%async_computation.4 | async-start | bytes 524288 | tf_op jit(solution)/shard_map/while/body/eval_jaxpr/all_to_all | solution.py:143
  1355.5 17.7 %all-to-all-start.1 = ((bf16[16,4,2048]{2,1,0:T(4,128)(2,1)}), bf16[16,4,2048]{2,1,0:T(4,128)(2,1)}, u32[]{:S(2)}, u32[]{:S(2)}) async-start(bf16[16,4,2048]{2,1,0:T(4,128)(2,1)} %reshape.177), calls=%async_computation.1 | async-start | bytes 524288 | tf_op jit(solution)/shard_map/while/body/eval_jaxpr/all_to_all | solution.py:130
  1373.2 19.9 %all-to-all-start.4 = ((bf16[16,4,2048]{2,1,0:T(4,128)(2,1)}), bf16[16,4,2048]{2,1,0:T(4,128)(2,1)S(1)}, u32[]{:S(2)}, u32[]{:S(2)}) async-start(bf16[16,4,2048]{2,1,0:T(4,128)(2,1)} %reshape.183), calls=%async_computation.4 | async-start | bytes 524288 | tf_op jit(solution)/shard_map/while/body/eval_jaxpr/all_to_all | solution.py:143
  1379.7 16.8 collective-permute-start
  1405.4 18.1 %all-to-all-start = ((bf16[16,4,2048]{2,1,0:T(4,128)(2,1)}), bf16[16,4,2048]{2,1,0:T(4,128)(2,1)S(1)}, u32[]{:S(2)}, u32[]{:S(2)}) async-start(bf16[16,4,2048]{2,1,0:T(4,128)(2,1)} %reshape.175), calls=%async_computation | async-start | bytes 524288 | tf_op jit(solution)/shard_map/while/body/eval_jaxpr/all_to_all | solution.py:132
  1456.0 17.7 %all-to-all-start.1 = ((bf16[16,4,2048]{2,1,0:T(4,128)(2,1)}), bf16[16,4,2048]{2,1,0:T(4,128)(2,1)}, u32[]{:S(2)}, u32[]{:S(2)}) async-start(bf16[16,4,2048]{2,1,0:T(4,128)(2,1)} %reshape.177), calls=%async_computation.1 | async-start | bytes 524288 | tf_op jit(solution)/shard_map/while/body/eval_jaxpr/all_to_all | solution.py:130
  1473.7 20.0 %all-to-all-start.4 = ((bf16[16,4,2048]{2,1,0:T(4,128)(2,1)}), bf16[16,4,2048]{2,1,0:T(4,128)(2,1)S(1)}, u32[]{:S(2)}, u32[]{:S(2)}) async-start(bf16[16,4,2048]{2,1,0:T(4,128)(2,1)} %reshape.183), calls=%async_computation.4 | async-start | bytes 524288 | tf_op jit(solution)/shard_map/while/body/eval_jaxpr/all_to_all | solution.py:143
  1553.8 17.7 %all-to-all-start.1 = ((bf16[16,4,2048]{2,1,0:T(4,128)(2,1)}), bf16[16,4,2048]{2,1,0:T(4,128)(2,1)}, u32[]{:S(2)}, u32[]{:S(2)}) async-start(bf16[16,4,2048]{2,1,0:T(4,128)(2,1)} %reshape.177), calls=%async_computation.1 | async-start | bytes 524288 | tf_op jit(solution)/shard_map/while/body/eval_jaxpr/all_to_all | solution.py:130
  1571.5 19.8 %all-to-all-start.4 = ((bf16[16,4,2048]{2,1,0:T(4,128)(2,1)}), bf16[16,4,2048]{2,1,0:T(4,128)(2,1)S(1)}, u32[]{:S(2)}, u32[]{:S(2)}) async-start(bf16[16,4,2048]{2,1,0:T(4,128)(2,1)} %reshape.183), calls=%async_computation.4 | async-start | bytes 524288 | tf_op jit(solution)/shard_map/while/body/eval_jaxpr/all_to_all | solution.py:143
  1577.9 16.8 collective-permute-start
  1603.6 18.2 %all-to-all-start = ((bf16[16,4,2048]{2,1,0:T(4,128)(2,1)}), bf16[16,4,2048]{2,1,0:T(4,128)(2,1)S(1)}, u32[]{:S(2)}, u32[]{:S(2)}) async-start(bf16[16,4,2048]{2,1,0:T(4,128)(2,1)} %reshape.175), calls=%async_computation | async-start | bytes 524288 | tf_op jit(solution)/shard_map/while/body/eval_jaxpr/all_to_all | solution.py:132
  1654.2 17.7 %all-to-all-start.1 = ((bf16[16,4,2048]{2,1,0:T(4,128)(2,1)}), bf16[16,4,2048]{2,1,0:T(4,128)(2,1)}, u32[]{:S(2)}, u32[]{:S(2)}) async-start(bf16[16,4,2048]{2,1,0:T(4,128)(2,1)} %reshape.177), calls=%async_computation.1 | async-start | bytes 524288 | tf_op jit(solution)/shard_map/while/body/eval_jaxpr/all_to_all | solution.py:130
  1671.9 20.0 %all-to-all-start.4 = ((bf16[16,4,2048]{2,1,0:T(4,128)(2,1)}), bf16[16,4,2048]{2,1,0:T(4,128)(2,1)S(1)}, u32[]{:S(2)}, u32[]{:S(2)}) async-start(bf16[16,4,2048]{2,1,0:T(4,128)(2,1)} %reshape.183), calls=%async_computation.4 | async-start | bytes 524288 | tf_op jit(solution)/shard_map/while/body/eval_jaxpr/all_to_all | solution.py:143
  (446 other events, 6876.0 us)
where the time goes:
time: 1710 us; the launch traced here: 1700 us
  waiting for transfers between devices  697 us (41%)
  starting transfers between devices  512 us (30%)
  matrix products  262 us (15%)
  local copies, waits for them, and re-layouts  173 us (10%)
  other arithmetic  46.5 us (3%)
    all_to_all x17, waiting for transfers between devices, layer_work(): lax.all_to_all(send_forward, 'expert', split_axis=0, concat_axis=0, tiled...  207 us
    all_to_all x17, waiting for transfers between devices, layer_work(): lax.all_to_all(backward_rows(rows_backward, rows_sent), 'expert', split_a...  142 us
    all_to_all x17, waiting for transfers between devices, layer_work(): lax.all_to_all(send_grads, 'expert', split_axis=0, concat_axis=0, tiled=T...  133 us
    ppermute x34, starting transfers between devices, from_behind(): return lax.ppermute(array, axis, pairs)  121 us
    all_to_all x17, starting transfers between devices, layer_work(): lax.all_to_all(forward_rows(lax.all_to_all(send_forward, 'expert', split_...  95.8 us
    all_to_all x17, starting transfers between devices, layer_work(): lax.all_to_all(backward_rows(rows_backward, rows_sent), 'expert', split_a...  85.9 us
    all_to_all x17, waiting for transfers between devices, layer_work(): lax.all_to_all(forward_rows(lax.all_to_all(send_forward, 'expert', split_...  79.4 us
    all_to_all x17, starting transfers between devices, layer_work(): lax.all_to_all(send_saved, 'expert', split_axis=0, concat_axis=0, tiled=T...  71.3 us
  transfers between devices with their start and end apart: 119, of which 102 were waited for; matrix products, arithmetic and copies ran while one was open for 23% of the time, Pallas kernels for 0%

commit v1 on v0

v1 whole, which is shorter than its diff:
```python
import functools

import jax
import jax.numpy as jnp
from jax import lax
from jax.experimental import pallas as pl
from jax.experimental.pallas import tpu as pltpu
from jax.sharding import PartitionSpec as P

EPSILON = 1e-06
MESH = pl.DeviceIdType.MESH
F32 = jnp.float32
BF16 = jnp.bfloat16
ROWS = 16


def iota(shape, dim):
    return lax.broadcasted_iota(jnp.int32, shape, dim)


def dot(a, b):
    return jnp.dot(a, b, preferred_element_type=F32)


def dot_nt(a, b):
    return lax.dot_general(a, b, (((1,), (1,)), ((), ())), preferred_element_type=F32)


def dot_tn(a, b):
    return lax.dot_general(a, b, (((0,), (0,)), ((), ())), preferred_element_type=F32)


def kernel(
    sizes,
    entering,
    cotangent,
    saved,
    gain_f,
    gain_b,
    route_f,
    route_b,
    share_f,
    share_b,
    gate_f,
    up_f,
    down_f,
    gate_b,
    up_b,
    down_b,
    out_f,
    out_b,
    gu_f,
    dn_f,
    gu_b,
    dn_b,
    ein,
    eout,
    rin,
    rout,
    disp,
    sdisp,
    sin,
    msend,
    mrecv,
    mflat,
    csend,
    crecv,
    perm,
    permt,
    rmat,
    aexp,
    vrows,
    fact1,
    fact2,
    rsaved,
    w_sem,
    ein_sem,
    rin_sem,
    sin_sem,
    m_sem,
    c_sem,
    eout_sem,
    rout_sem,
    disp_sem,
    sdisp_sem,
    msend_sem,
    csend_sem,
):
    stages, group, micro, tokens, width, hidden_width, cap = sizes
    parts = ROWS // cap
    wide = width // parts
    rows = group * cap
    total = group * ROWS
    chains = 2 * micro
    stage = lax.axis_index("pipe")
    me = lax.axis_index("expert")
    first = stage == 0
    last = stage == stages - 1

    weights = [
        (gate_f.at[0, 0], gu_f.at[:, 0:hidden_width]),
        (up_f.at[0, 0], gu_f.at[:, hidden_width : 2 * hidden_width]),
        (down_f.at[0, 0], dn_f),
        (gate_b.at[0, 0], gu_b.at[:, 0:hidden_width]),
        (up_b.at[0, 0], gu_b.at[:, hidden_width : 2 * hidden_width]),
        (down_b.at[0, 0], dn_b),
    ]
    loads = [pltpu.make_async_copy(s, d, w_sem.at[i]) for i, (s, d) in enumerate(weights)]
    for load in (loads[3], loads[4], loads[0], loads[1], loads[2], loads[5]):
        load.start()

    barrier = pltpu.get_barrier_semaphore()

    def greet(pipe, peer):
        pl.semaphore_signal(barrier, inc=1, device_id=(pipe, peer), device_id_type=MESH)

    def greet_group(i, carry):
        greet(stage, lax.rem(me + i, group))
        return carry

    lax.fori_loop(1, group, greet_group, 0)

    @pl.when(stage > 0)
    def _():
        def greet_before(i, carry):
            greet(stage - 1, lax.rem(me + i, group))
            return carry

        lax.fori_loop(0, group, greet_before, 0)

    @pl.when(stage < stages - 1)
    def _():
        greet(stage + 1, me)

    def column_to_row(column):
        eye = iota((tokens, tokens), 0) == iota((tokens, tokens), 1)
        return jnp.sum(jnp.where(eye, column, 0.0), axis=0, keepdims=True)

    def row_to_column(row):
        eye = iota((tokens, tokens), 0) == iota((tokens, tokens), 1)
        return jnp.sum(jnp.where(eye, row, 0.0), axis=1, keepdims=True)

    def code_of(route_column):
        member = (iota((tokens, 128), 1) == route_column).astype(BF16)
        same = dot_nt(member, member)
        before = iota((tokens, tokens), 1) < iota((tokens, tokens), 0)
        slot = jnp.sum(jnp.where(before, same, 0.0), axis=1, keepdims=True)
        return route_column.astype(F32) * ROWS + slot

    def expanded(code):
        column = jnp.concatenate([code + q * cap for q in range(parts)], axis=0)
        return (iota((parts * tokens, total), 1).astype(F32) == column).astype(BF16)

    codes = []
    for micro_index in range(micro):
        for route in (route_f, route_b):
            codes.append(code_of(route[0, micro_index]))
    for c in range(chains):
        aexp[c] = expanded(codes[c])

    def chunk_row(index):
        return lax.rem(index, rows) // cap * ROWS + index // rows * cap + lax.rem(index, cap)

    perm[...] = (iota((total, total), 1) == chunk_row(iota((total, total), 0))).astype(BF16)
    permt[...] = (iota((total, total), 0) == chunk_row(iota((total, total), 1))).astype(BF16)

    def stacked(values):
        return jnp.concatenate([values[:, q * wide : (q + 1) * wide] for q in range(parts)], axis=0)

    def scatter(c, values):
        return dot_tn(aexp[c], stacked(values)).astype(BF16).reshape(group, ROWS, wide)

    def send_chunks(source, target, pipe, send_sem, recv_sem, begin):
        def send(i, carry):
            peer = lax.rem(me + i, group)
            pltpu.make_async_remote_copy(
                src_ref=source.at[peer],
                dst_ref=target.at[me],
                send_sem=send_sem,
                recv_sem=recv_sem,
                device_id=(pipe, peer),
                device_id_type=MESH,
            ).start()
            return carry

        lax.fori_loop(begin, group, send, 0)

    def send_group(source, target, send_sem, recv_sem):
        send_chunks(source, target, stage, send_sem, recv_sem, 1)
        pltpu.make_async_copy(source.at[me], target.at[me], recv_sem).start()

    def wait_bytes(ref, sem):
        pltpu.make_async_copy(ref, ref, sem).wait()

    greeted = group - 1 + jnp.where(last, 0, group) + jnp.where(first, 0, 1)
    pl.semaphore_wait(barrier, greeted)

    @pl.when(first)
    def _():
        for c in range(chains):
            source = entering if c % 2 == 0 else cotangent
            disp[c] = scatter(c, source[c // 2])
            send_group(disp.at[c], ein.at[c], disp_sem.at[c], ein_sem.at[c])

    for direction, share in ((0, share_f), (1, share_b)):
        column = jnp.zeros((rows * micro, 1), F32)
        for micro_index in range(micro):
            code_row = column_to_row(codes[2 * micro_index + direction])
            index = iota((rows * micro, tokens), 0)
            row_code = index // (cap * micro) * ROWS + lax.rem(index, cap * micro) // micro
            hit = jnp.logical_and(
                row_code.astype(F32) == code_row, lax.rem(index, micro) == micro_index
            )
            share_row = share[0, micro_index : micro_index + 1]
            column = column + jnp.sum(jnp.where(hit, share_row, 0.0), axis=1, keepdims=True)
        msend[:, :, direction * 64 : direction * 64 + 64] = jnp.broadcast_to(
            column, (rows * micro, 64)
        ).reshape(group, cap * micro, 64)
    send_group(msend, mrecv, msend_sem, m_sem)

    for micro_index in range(micro):
        sdisp[micro_index] = scatter(2 * micro_index + 1, saved[0, micro_index])
        send_group(
            sdisp.at[micro_index], sin.at[micro_index], sdisp_sem.at[micro_index], sin_sem.at[micro_index]
        )

    lane = iota((tokens, 128), 1)
    packed = jnp.zeros((tokens, 128), F32)
    for c in range(chains):
        packed = packed + jnp.where(lane == c, codes[c], 0.0)
    csend[...] = packed

    def code_copy():
        return pltpu.make_async_remote_copy(
            src_ref=csend,
            dst_ref=crecv,
            send_sem=csend_sem,
            recv_sem=c_sem,
            device_id=(lax.rem(stage + stages - 1, stages), me),
            device_id_type=MESH,
        )

    @pl.when(stage > 0)
    def _():
        code_copy().start()

    def arrange(chunks):
        return dot(perm[...], chunks.reshape(total, wide))

    def part(values, q):
        return values[q * rows : (q + 1) * rows]

    def gain_part(gain, q):
        return gain[:, q * wide : (q + 1) * wide]

    def row_sum(values, weigh):
        result = jnp.zeros((rows, 1), F32)
        for q in range(parts):
            result = result + jnp.sum(weigh(q, part(values, q)), axis=1, keepdims=True)
        return result

    def inverse_scale(values):
        squares = row_sum(values, lambda q, v: v * v) * (1.0 / width)
        return lax.rsqrt(squares + EPSILON)

    def normed(values, inverse, gain):
        return jnp.concatenate(
            [(part(values, q) * inverse * gain_part(gain, q)).astype(BF16) for q in range(parts)],
            axis=1,
        )

    def share_of(micro_index, direction):
        lanes = mflat[pl.ds(micro_index, rows, stride=micro), :]
        return lanes[:, direction * 64 : direction * 64 + 1]

    def finish(c, values):
        eout[c] = dot(permt[...], values).astype(BF16).reshape(group, ROWS, wide)
        send_group(eout.at[c], rin.at[c], eout_sem.at[c], rin_sem.at[c])

    def expert_forward(micro_index):
        c = 2 * micro_index
        wait_bytes(ein.at[c], ein_sem.at[c])
        x = arrange(ein[c])
        gain = gain_f[...]
        pre = dot(normed(x, inverse_scale(x), gain), gu_f[...])
        pre_gate, pre_up = pre[:, :hidden_width], pre[:, hidden_width:]
        hidden = (pre_gate / (1.0 + jnp.exp(-pre_gate)) * pre_up).astype(BF16)
        out = dot(hidden, dn_f[...]).astype(BF16).astype(F32)
        share = share_of(micro_index, 0)
        finish(
            c,
            jnp.concatenate(
                [
                    (part(x, q) + share * out[:, q * wide : (q + 1) * wide]).astype(BF16)
                    for q in range(parts)
                ],
                axis=0,
            ),
        )

    def prepare_backward(micro_index):
        wait_bytes(sin.at[micro_index], sin_sem.at[micro_index])
        v = arrange(sin[micro_index])
        vrows[micro_index] = v.astype(BF16)
        inverse = inverse_scale(v)
        rsaved[micro_index] = jnp.broadcast_to(inverse, (rows, 128))
        back = dot(normed(v, inverse, gain_b[...]), gu_b[...])
        back_gate, back_up = back[:, :hidden_width], back[:, hidden_width:]
        s = 1.0 / (1.0 + jnp.exp(-back_gate))
        fact1[micro_index] = back_up * s * (1.0 + back_gate * (1.0 - s))
        fact2[micro_index] = back_gate * s

    def expert_backward(micro_index):
        c = 2 * micro_index + 1
        wait_bytes(ein.at[c], ein_sem.at[c])
        dy = arrange(ein[c])
        share = share_of(micro_index, 1)
        sent = jnp.concatenate(
            [(share * part(dy, q)).astype(BF16) for q in range(parts)], axis=1
        )
        d_hidden = dot_nt(sent, dn_b[...])
        both = jnp.concatenate(
            [
                (d_hidden * fact1[micro_index]).astype(BF16),
                (d_hidden * fact2[micro_index]).astype(BF16),
            ],
            axis=1,
        )
        d_rows = dot_nt(both, gu_b[...]).astype(BF16).astype(F32)
        inverse = rsaved[micro_index][:, 0:1]
        gain = gain_b[...]
        scaled = [d_rows[:, q * wide : (q + 1) * wide] * gain_part(gain, q) for q in range(parts)]
        v = [vrows[micro_index, q * rows : (q + 1) * rows].astype(F32) for q in range(parts)]
        inner = jnp.zeros((rows, 1), F32)
        for q in range(parts):
            inner = inner + jnp.sum(scaled[q] * v[q], axis=1, keepdims=True)
        back = inner * (1.0 / width) * inverse * inverse * inverse
        finish(
            c,
            jnp.concatenate(
                [
                    (part(dy, q) + (scaled[q] * inverse - v[q] * back)).astype(BF16)
                    for q in range(parts)
                ],
                axis=0,
            ),
        )

    def relay(c):
        wait_bytes(rin.at[c], rin_sem.at[c])

        @pl.when(stage < stages - 1)
        def _():
            moved = dot(rmat[c], rin[c].reshape(total, wide))
            rout[c] = moved.astype(BF16).reshape(group, ROWS, wide)
            send_chunks(rout.at[c], ein.at[c], stage + 1, rout_sem.at[c], ein_sem.at[c], 0)

        kept = dot(aexp[c], rin[c].reshape(total, wide)).astype(BF16)
        out = out_f if c % 2 == 0 else out_b
        for q in range(parts):
            out[0, c // 2, :, q * wide : (q + 1) * wide] = kept[q * tokens : (q + 1) * tokens]

    wait_bytes(mrecv, m_sem)
    mflat[...] = mrecv[...].reshape(rows * micro, 128)
    loads[3].wait()
    loads[4].wait()
    for micro_index in range(micro):
        prepare_backward(micro_index)

    @pl.when(stage < stages - 1)
    def _():
        code_copy().wait_recv()
        for c in range(chains):
            rmat[c] = dot_tn(expanded(crecv[:, c : c + 1]), aexp[c]).astype(BF16)

    for i in (0, 1, 2, 5):
        loads[i].wait()

    expert_forward(0)
    expert_backward(0)
    expert_forward(1)
    relay(0)
    expert_backward(1)
    relay(1)
    relay(2)
    relay(3)

    @pl.when(stage > 0)
    def _():
        code_copy().wait_send()

    wait_bytes(msend.at[pl.ds(0, group - 1)], msend_sem)
    for micro_index in range(micro):
        wait_bytes(sdisp.at[micro_index, pl.ds(0, group - 1)], sdisp_sem.at[micro_index])
    for c in range(chains):
        wait_bytes(eout.at[c, pl.ds(0, group - 1)], eout_sem.at[c])

    @pl.when(first)
    def _():
        for c in range(chains):
            wait_bytes(disp.at[c, pl.ds(0, group - 1)], disp_sem.at[c])

    @pl.when(stage < stages - 1)
    def _():
        for c in range(chains):
            wait_bytes(rout.at[c], rout_sem.at[c])


def solution(mesh):
    stages, group = mesh.shape["pipe"], mesh.shape["expert"]

    def local(
        entering,
        first_gain,
        first_gate,
        first_up,
        first_down,
        first_route,
        first_share,
        saved_inputs,
        cotangent,
        second_gain,
        second_gate,
        second_up,
        second_down,
        second_route,
        second_share,
    ):
        micro, tokens, width = entering.shape
        hidden_width = first_gate.shape[-1]
        cap = 2 * tokens // group
        parts = ROWS // cap
        wide = width // parts
        rows, total, chains = group * cap, group * ROWS, 2 * micro
        vmem = pl.BlockSpec(memory_space=pltpu.VMEM)
        anywhere = pl.BlockSpec(memory_space=pl.ANY)
        dma = pltpu.SemaphoreType.DMA
        chunks = lambda count: pltpu.VMEM((count, group, ROWS, wide), BF16)
        state = jax.ShapeDtypeStruct((1, micro, tokens, width), BF16)
        return pl.pallas_call(
            functools.partial(
                kernel, (stages, group, micro, tokens, width, hidden_width, cap)
            ),
            out_shape=(state, state),
            in_specs=[vmem] * 9 + [anywhere] * 6,
            out_specs=(vmem, vmem),
            scratch_shapes=[
                pltpu.VMEM((width, 2 * hidden_width), BF16),
                pltpu.VMEM((hidden_width, width), BF16),
                pltpu.VMEM((width, 2 * hidden_width), BF16),
                pltpu.VMEM((hidden_width, width), BF16),
                chunks(chains),
                chunks(chains),
                chunks(chains),
                chunks(chains),
                chunks(chains),
                chunks(micro),
                chunks(micro),
                pltpu.VMEM((group, cap * micro, 128), F32),
                pltpu.VMEM((group, cap * micro, 128), F32),
                pltpu.VMEM((rows * micro, 128), F32),
                pltpu.VMEM((tokens, 128), F32),
                pltpu.VMEM((tokens, 128), F32),
                pltpu.VMEM((total, total), BF16),
                pltpu.VMEM((total, total), BF16),
                pltpu.VMEM((chains, total, total), BF16),
                pltpu.VMEM((chains, parts * tokens, total), BF16),
                pltpu.VMEM((micro, total, wide), BF16),
                pltpu.VMEM((micro, rows, hidden_width), F32),
                pltpu.VMEM((micro, rows, hidden_width), F32),
                pltpu.VMEM((micro, rows, 128), F32),
                dma((6,)),
                dma((chains,)),
                dma((chains,)),
                dma((micro,)),
                dma,
                dma,
                dma((chains,)),
                dma((chains,)),
                dma((chains,)),
                dma((micro,)),
                dma,
                dma,
            ],
            compiler_params=pltpu.CompilerParams(
                collective_id=0, has_side_effects=True, vmem_limit_bytes=48 * 1024 * 1024
            ),
        )(
            entering,
            cotangent,
            saved_inputs,
            first_gain,
            second_gain,
            first_route,
            second_route,
            first_share,
            second_share,
            first_gate,
            first_up,
            first_down,
            second_gate,
            second_up,
            second_down,
        )

    return jax.shard_map(
        local,
        mesh=mesh,
        in_specs=(
            P(None, "expert", None),
            P("pipe", None),
            P("pipe", "expert", None, None),
            P("pipe", "expert", None, None),
            P("pipe", "expert", None, None),
            P("pipe", None, "expert", None),
            P("pipe", None, "expert"),
            P("pipe", None, "expert", None),
            P(None, "expert", None),
            P("pipe", None),
            P("pipe", "expert", None, None),
            P("pipe", "expert", None, None),
            P("pipe", "expert", None, None),
            P("pipe", None, "expert", None),
            P("pipe", None, "expert"),
        ),
        out_specs=(P("pipe", None, "expert", None), P("pipe", None, "expert", None)),
        check_vma=False,
    )
```

time: 1710 us -> 470 us (0.27)
  the two profiles are of different devices: /device:TPU:40 before, /device:TPU:121 now
where the time goes in v1:
time: 470 us
  Pallas kernels  456 us (97%)
  local copies, waits for them, and re-layouts  12.8 us (3%)
    pallas_call x1, Pallas kernels, local(): pl.pallas_call(functools.partial(kernel, (stages, group, micro, tokens, w...  456 us
    unnamed x24, local copies, waits for them, and re-layouts  12.8 us

profile of v1, /device:TPU:121, one launch (start us, length us, event | category | flops | bytes accessed | tf_op | source)
XLA Modules:
  0.0 469.9 jit_solution(3639434186089522573)
XLA Ops:
  0.6 0.8 copy.17.route_f
  1.4 0.8 copy.18.route_b
  2.2 0.0 copy-start
  2.2 1.4 copy-done
  3.6 0.0 copy-start.1
  3.6 1.4 copy-done.1
  5.0 0.0 copy-start.2
  5.0 1.4 copy-done.2
  6.4 0.0 copy-start.3
  6.4 0.9 copy-done.3
  7.3 0.0 copy-start.4
  7.3 0.9 copy-done.4
  8.3 0.0 copy-start.5
  8.3 0.9 copy-done.5
  9.2 0.0 copy-start.6
  9.2 0.7 copy-done.6
  9.9 0.0 copy-start.7
  9.9 0.7 copy-done.7
  10.6 0.0 copy-start.8
  10.6 0.7 copy-done.8
  11.3 0.0 copy-start.9
  11.3 0.7 copy-done.9
  12.0 456.5 %shard_map.158 = (bf16[1,2,32,2048]{3,2,1,0:T(8,128)(2,1)S(1)}, bf16[1,2,32,2048]{3,2,1,0:T(8,128)(2,1)S(1)}) custom-call(bf16[2,32,2048]{2,1,0:T(8,128)(2,1)S(1)} %copy-done.3, bf16[2,32,2048]{2,1,0:T(8,128)(2,1)S(1)} %copy-done.4, bf16[1,2,32,2048]{3,2,1,0:T(8,128)(2,1)S(1)} %copy-done.5, f32[1,2048]{1,0:T(1,128)S(1)} %copy-done.6, ...), custom_call_target="tpu_custom_call" | custom-call | tf_op jit(solution)/shard_map/pallas_call | solution.py:440
  468.5 0.7 copy.21
  469.2 0.7 copy.22
Async XLA Ops:
  2.2 1.4 copy-start
  3.6 1.4 copy-start.1
  5.0 1.4 copy-start.2
  6.4 0.9 copy-start.3
  7.3 0.9 copy-start.4
  8.3 0.9 copy-start.5
  9.2 0.7 copy-start.6
  9.9 0.7 copy-start.7
  10.6 0.7 copy-start.8
  11.3 0.7 copy-start.9

commit v2 on v1

--- a/solution.py
+++ b/solution.py
@@ -12,6 +12,19 @@
 F32 = jnp.float32
 BF16 = jnp.bfloat16
 ROWS = 16
+NEAR = 4
+
+
+def shift_of(block):
+    return jnp.where(block % 4 == 1, NEAR, 0) - jnp.where(block % 4 == 3, NEAR, 0)
+
+
+def relay_of(stage, block, stages):
+    return lax.rem(stage + shift_of(block) + stages, stages)
+
+
+def relayed_by(place, block, stages):
+    return lax.rem(place - shift_of(block) + stages, stages)
 
 
 def iota(shape, dim):
@@ -63,8 +76,10 @@
     msend,
     mrecv,
     mflat,
+    shares,
     csend,
     crecv,
+    cnext,
     perm,
     permt,
     rmat,
@@ -73,18 +88,23 @@
     fact1,
     fact2,
     rsaved,
+    kept,
     w_sem,
     ein_sem,
     rin_sem,
     sin_sem,
     m_sem,
     c_sem,
+    cnext_sem,
+    out_sem,
     eout_sem,
     rout_sem,
     disp_sem,
     sdisp_sem,
     msend_sem,
     csend_sem,
+    cnsend_sem,
+    kept_sem,
 ):
     stages, group, micro, tokens, width, hidden_width, cap = sizes
     parts = ROWS // cap
@@ -95,7 +115,10 @@
     stage = lax.axis_index("pipe")
     me = lax.axis_index("expert")
     first = stage == 0
-    last = stage == stages - 1
+    host = relay_of(stage, me, stages)
+    source_stage = relayed_by(stage, me, stages)
+    has_next = source_stage < stages - 1
+    at_home = host == stage
 
     weights = [
         (gate_f.at[0, 0], gu_f.at[:, 0:hidden_width]),
@@ -120,17 +143,27 @@
 
     lax.fori_loop(1, group, greet_group, 0)
 
+    @pl.when(jnp.logical_not(at_home))
+    def _():
+        def greet_source(i, carry):
+            greet(source_stage, lax.rem(me + i, group))
+            return carry
+
+        lax.fori_loop(0, group, greet_source, 0)
+        greet(host, me)
+
     @pl.when(stage > 0)
     def _():
         def greet_before(i, carry):
-            greet(stage - 1, lax.rem(me + i, group))
+            peer = lax.rem(me + i, group)
+            greet(relay_of(stage - 1, peer, stages), peer)
             return carry
 
         lax.fori_loop(0, group, greet_before, 0)
 
-    @pl.when(stage < stages - 1)
-    def _():
-        greet(stage + 1, me)
+    @pl.when(has_next)
+    def _():
+        greet(source_stage + 1, me)
 
     def column_to_row(column):
         eye = iota((tokens, tokens), 0) == iota((tokens, tokens), 1)
@@ -155,9 +188,6 @@
     for micro_index in range(micro):
         for route in (route_f, route_b):
             codes.append(code_of(route[0, micro_index]))
-    for c in range(chains):
-        aexp[c] = expanded(codes[c])
-
     def chunk_row(index):
         return lax.rem(index, rows) // cap * ROWS + index // rows * cap + lax.rem(index, cap)
 
@@ -167,40 +197,53 @@
     def stacked(values):
         return jnp.concatenate([values[:, q * wide : (q + 1) * wide] for q in range(parts)], axis=0)
 
-    def scatter(c, values):
-        return dot_tn(aexp[c], stacked(values)).astype(BF16).reshape(group, ROWS, wide)
-
-    def send_chunks(source, target, pipe, send_sem, recv_sem, begin):
+    def scatter(table, values):
+        return dot_tn(table, stacked(values)).astype(BF16).reshape(group, ROWS, wide)
+
+    def send_chunks(source, target, pipe_of, far, count, send_sem, recv_sem):
         def send(i, carry):
-            peer = lax.rem(me + i, group)
+            across, j = i // 8, i % 8 // 2
+            step_x = jnp.where(j < 2, 2 + j, 3 - j)
+            peer = (
+                (me // 4 + step_x) % 4 * 4 + (me % 4 // 2 + far + across) % 2 * 2 + (me + 1 + i) % 2
+            )
             pltpu.make_async_remote_copy(
                 src_ref=source.at[peer],
                 dst_ref=target.at[me],
                 send_sem=send_sem,
                 recv_sem=recv_sem,
-                device_id=(pipe, peer),
+                device_id=(pipe_of(peer), peer),
                 device_id_type=MESH,
             ).start()
             return carry
 
-        lax.fori_loop(begin, group, send, 0)
+        lax.fori_loop(0, count, send, 0)
 
     def send_group(source, target, send_sem, recv_sem):
-        send_chunks(source, target, stage, send_sem, recv_sem, 1)
+        send_chunks(source, target, lambda peer: stage, 1, group - 1, send_sem, recv_sem)
         pltpu.make_async_copy(source.at[me], target.at[me], recv_sem).start()
 
     def wait_bytes(ref, sem):
         pltpu.make_async_copy(ref, ref, sem).wait()
 
-    greeted = group - 1 + jnp.where(last, 0, group) + jnp.where(first, 0, 1)
+    greeted = (
+        group - 1
+        + group // 2
+        + jnp.where(has_next, group, 0)
+        + jnp.where(first, 0, 1)
+        + jnp.where(at_home, 0, 1)
+    )
     pl.semaphore_wait(barrier, greeted)
 
+    def deal(micro_index):
+        for c in (2 * micro_index, 2 * micro_index + 1):
+            source = entering if c % 2 == 0 else cotangent
+            disp[c] = scatter(expanded(codes[c]), source[micro_index])
+            send_group(disp.at[c], ein.at[c], disp_sem.at[c], ein_sem.at[c])
+
     @pl.when(first)
     def _():
-        for c in range(chains):
-            source = entering if c % 2 == 0 else cotangent
-            disp[c] = scatter(c, source[c // 2])
-            send_group(disp.at[c], ein.at[c], disp_sem.at[c], ein_sem.at[c])
+        deal(0)
 
     for direction, share in ((0, share_f), (1, share_b)):
         column = jnp.zeros((rows * micro, 1), F32)
@@ -219,7 +262,7 @@
     send_group(msend, mrecv, msend_sem, m_sem)
 
     for micro_index in range(micro):
-        sdisp[micro_index] = scatter(2 * micro_index + 1, saved[0, micro_index])
+        sdisp[micro_index] = scatter(expanded(codes[2 * micro_index + 1]), saved[0, micro_index])
         send_group(
             sdisp.at[micro_index], sin.at[micro_index], sdisp_sem.at[micro_index], sin_sem.at[micro_index]
         )
@@ -230,19 +273,27 @@
         packed = packed + jnp.where(lane == c, codes[c], 0.0)
     csend[...] = packed
 
-    def code_copy():
+    def code_copy(target, send_sem, recv_sem, pipe):
         return pltpu.make_async_remote_copy(
             src_ref=csend,
-            dst_ref=crecv,
-            send_sem=csend_sem,
-            recv_sem=c_sem,
-            device_id=(lax.rem(stage + stages - 1, stages), me),
+            dst_ref=target,
+            send_sem=send_sem,
+            recv_sem=recv_sem,
+            device_id=(pipe, me),
             device_id_type=MESH,
         )
 
+    @pl.when(at_home)
+    def _():
+        pltpu.make_async_copy(csend, crecv, c_sem).start()
+
+    @pl.when(jnp.logical_not(at_home))
+    def _():
+        code_copy(crecv, csend_sem, c_sem, host).start()
+
     @pl.when(stage > 0)
     def _():
-        code_copy().start()
+        code_copy(cnext, cnsend_sem, cnext_sem, relay_of(stage - 1, me, stages)).start()
 
     def arrange(chunks):
         return dot(perm[...], chunks.reshape(total, wide))
@@ -269,13 +320,32 @@
             axis=1,
         )
 
-    def share_of(micro_index, direction):
-        lanes = mflat[pl.ds(micro_index, rows, stride=micro), :]
-        return lanes[:, direction * 64 : direction * 64 + 1]
-
     def finish(c, values):
         eout[c] = dot(permt[...], values).astype(BF16).reshape(group, ROWS, wide)
-        send_group(eout.at[c], rin.at[c], eout_sem.at[c], rin_sem.at[c])
+        send_chunks(
+            eout.at[c],
+            rin.at[c],
+            lambda peer: relay_of(stage, peer, stages),
+            1,
+            group - 1,
+            eout_sem.at[c],
+            rin_sem.at[c],
+        )
+
+        @pl.when(at_home)
+        def _():
+            pltpu.make_async_copy(eout.at[c, me], rin.at[c, me], rin_sem.at[c]).start()
+
+        @pl.when(jnp.logical_not(at_home))
+        def _():
+            pltpu.make_async_remote_copy(
+                src_ref=eout.at[c, me],
+                dst_ref=rin.at[c, me],
+                send_sem=eout_sem.at[c],
+                recv_sem=rin_sem.at[c],
+                device_id=(host, me),
+                device_id_type=MESH,
+            ).start()
 
     def expert_forward(micro_index):
         c = 2 * micro_index
@@ -286,7 +356,7 @@
         pre_gate, pre_up = pre[:, :hidden_width], pre[:, hidden_width:]
         hidden = (pre_gate / (1.0 + jnp.exp(-pre_gate)) * pre_up).astype(BF16)
         out = dot(hidden, dn_f[...]).astype(BF16).astype(F32)
-        share = share_of(micro_index, 0)
+        share = shares[c][:, 0:1]
         finish(
             c,
             jnp.concatenate(
@@ -314,7 +384,7 @@
         c = 2 * micro_index + 1
         wait_bytes(ein.at[c], ein_sem.at[c])
         dy = arrange(ein[c])
-        share = share_of(micro_index, 1)
+        share = shares[c][:, 0:1]
         sent = jnp.concatenate(
             [(share * part(dy, q)).astype(BF16) for q in range(parts)], axis=1
         )
@@ -346,61 +416,121 @@
             ),
         )
 
-    def relay(c):
+    def relay(micro_index, direction):
+        c = 2 * micro_index + direction
         wait_bytes(rin.at[c], rin_sem.at[c])
 
-        @pl.when(stage < stages - 1)
+        @pl.when(has_next)
         def _():
             moved = dot(rmat[c], rin[c].reshape(total, wide))
             rout[c] = moved.astype(BF16).reshape(group, ROWS, wide)
-            send_chunks(rout.at[c], ein.at[c], stage + 1, rout_sem.at[c], ein_sem.at[c], 0)
-
-        kept = dot(aexp[c], rin[c].reshape(total, wide)).astype(BF16)
-        out = out_f if c % 2 == 0 else out_b
+            send_chunks(
+                rout.at[c],
+                ein.at[c],
+                lambda peer: source_stage + 1,
+                jnp.where(source_stage % NEAR == NEAR - 1, 0, 1),
+                group,
+                rout_sem.at[c],
+                ein_sem.at[c],
+            )
+
+        rows_kept = dot(aexp[c], rin[c].reshape(total, wide)).astype(BF16)
         for q in range(parts):
-            out[0, c // 2, :, q * wide : (q + 1) * wide] = kept[q * tokens : (q + 1) * tokens]
+            kept[c, :, q * wide : (q + 1) * wide] = rows_kept[q * tokens : (q + 1) * tokens]
+        out = (out_f, out_b)[direction].at[0, micro_index]
+
+        @pl.when(at_home)
+        def _():
+            pltpu.make_async_copy(kept.at[c], out, out_sem.at[c]).start()
+
+        @pl.when(jnp.logical_not(at_home))
+        def _():
+            pltpu.make_async_remote_copy(
+                src_ref=kept.at[c],
+                dst_ref=out,
+                send_sem=kept_sem.at[c],
+                recv_sem=out_sem.at[c],
+                device_id=(source_stage, me),
+                device_id_type=MESH,
+            ).start()
 
     wait_bytes(mrecv, m_sem)
     mflat[...] = mrecv[...].reshape(rows * micro, 128)
+    for micro_index in range(micro):
+        lanes = mflat[pl.ds(micro_index, rows, stride=micro), :]
+        for direction in range(2):
+            column = lanes[:, direction * 64 : direction * 64 + 1]
+            shares[2 * micro_index + direction] = jnp.broadcast_to(column, (rows, 128))
     loads[3].wait()
     loads[4].wait()
     for micro_index in range(micro):
         prepare_backward(micro_index)
 
-    @pl.when(stage < stages - 1)
-    def _():
-        code_copy().wait_recv()
+    wait_bytes(crecv, c_sem)
+    for c in range(chains):
+        aexp[c] = expanded(crecv[:, c : c + 1])
+
+    @pl.when(has_next)
+    def _():
+        wait_bytes(cnext, cnext_sem)
         for c in range(chains):
-            rmat[c] = dot_tn(expanded(crecv[:, c : c + 1]), aexp[c]).astype(BF16)
+            rmat[c] = dot_tn(expanded(cnext[:, c : c + 1]), aexp[c]).astype(BF16)
 
     for i in (0, 1, 2, 5):
         loads[i].wait()
 
-    expert_forward(0)
-    expert_backward(0)
-    expert_forward(1)
-    relay(0)
-    expert_backward(1)
-    relay(1)
-    relay(2)
-    relay(3)
+    def experts(micro_index):
+        expert_forward(micro_index)
+        expert_backward(micro_index)
+
+        @pl.when(jnp.logical_and(first, micro_index == 0))
+        def _():
+            deal(1)
+
+    def relays(micro_index):
+        relay(micro_index, 0)
+        relay(micro_index, 1)
+
+    def step(turn, carry):
+        odd, late = turn % 2, turn // 2
+        micro_index = jnp.where(at_home, late, odd)
+        second = jnp.where(at_home, odd, late)
+        is_relay = second == jnp.where(source_stage < stage, 0, 1)
+        pl.when(is_relay)(lambda: relays(micro_index))
+        pl.when(jnp.logical_not(is_relay))(lambda: experts(micro_index))
+        return carry
+
+    lax.fori_loop(0, 2 * micro, step, 0)
+
+    for c in range(chains):
+        wait_bytes((out_f if c % 2 == 0 else out_b).at[0, c // 2], out_sem.at[c])
+
+    @pl.when(at_home)
+    def _():
+        for c in range(chains):
+            wait_bytes(eout.at[c, pl.ds(0, group - 1)], eout_sem.at[c])
+
+    @pl.when(jnp.logical_not(at_home))
+    def _():
+        wait_bytes(csend, csend_sem)
+        for c in range(chains):
+            wait_bytes(kept.at[c], kept_sem.at[c])
+            wait_bytes(eout.at[c], eout_sem.at[c])
 
     @pl.when(stage > 0)
     def _():
-        code_copy().wait_send()
+        wait_bytes(csend, cnsend_sem)
 
     wait_bytes(msend.at[pl.ds(0, group - 1)], msend_sem)
     for micro_index in range(micro):
         wait_bytes(sdisp.at[micro_index, pl.ds(0, group - 1)], sdisp_sem.at[micro_index])
-    for c in range(chains):
-        wait_bytes(eout.at[c, pl.ds(0, group - 1)], eout_sem.at[c])
 
     @pl.when(first)
     def _():
         for c in range(chains):
             wait_bytes(disp.at[c, pl.ds(0, group - 1)], disp_sem.at[c])
 
-    @pl.when(stage < stages - 1)
+    @pl.when(has_next)
     def _():
         for c in range(chains):
             wait_bytes(rout.at[c], rout_sem.at[c])
@@ -459,6 +589,8 @@
                 pltpu.VMEM((group, cap * micro, 128), F32),
                 pltpu.VMEM((group, cap * micro, 128), F32),
                 pltpu.VMEM((rows * micro, 128), F32),
+                pltpu.VMEM((chains, rows, 128), F32),
+                pltpu.VMEM((tokens, 128), F32),
                 pltpu.VMEM((tokens, 128), F32),
                 pltpu.VMEM((tokens, 128), F32),
                 pltpu.VMEM((total, total), BF16),
@@ -469,18 +601,23 @@
                 pltpu.VMEM((micro, rows, hidden_width), F32),
                 pltpu.VMEM((micro, rows, hidden_width), F32),
                 pltpu.VMEM((micro, rows, 128), F32),
+                pltpu.VMEM((chains, tokens, width), BF16),
                 dma((6,)),
                 dma((chains,)),
                 dma((chains,)),
                 dma((micro,)),
                 dma,
                 dma,
+                dma,
+                dma((chains,)),
                 dma((chains,)),
                 dma((chains,)),
                 dma((chains,)),
                 dma((micro,)),
                 dma,
                 dma,
+                dma,
+                dma((chains,)),
             ],
             compiler_params=pltpu.CompilerParams(
                 collective_id=0, has_side_effects=True, vmem_limit_bytes=48 * 1024 * 1024

time: 470 us -> 328 us (0.70)
  Pallas kernels: 456 us -> 314 us
    pallas_call x1, Pallas kernels: 456 us -> 314 us  [local(): pl.pallas_call(functools.partial(kernel, (stages, group, micro, tokens, w...]
where the time goes in v2:
time: 328 us
  Pallas kernels  314 us (96%)
  local copies, waits for them, and re-layouts  12.8 us (4%)
    pallas_call x1, Pallas kernels, local(): pl.pallas_call(functools.partial(kernel, (stages, group, micro, tokens, w...  314 us
    unnamed x24, local copies, waits for them, and re-layouts  12.8 us

profile of v2, /device:TPU:121, one launch (start us, length us, event | category | flops | bytes accessed | tf_op | source)
XLA Modules:
  0.0 327.7 jit_solution(3864186136296542155)
XLA Ops:
  0.6 0.8 copy.17.route_f
  1.4 0.8 copy.18.route_b
  2.2 0.0 copy-start
  2.2 1.4 copy-done
  3.6 0.0 copy-start.1
  3.6 1.4 copy-done.1
  5.0 0.0 copy-start.2
  5.0 1.4 copy-done.2
  6.4 0.0 copy-start.3
  6.4 0.9 copy-done.3
  7.3 0.0 copy-start.4
  7.3 0.9 copy-done.4
  8.3 0.0 copy-start.5
  8.3 0.9 copy-done.5
  9.2 0.0 copy-start.6
  9.2 0.7 copy-done.6
  9.9 0.0 copy-start.7
  9.9 0.7 copy-done.7
  10.6 0.0 copy-start.8
  10.6 0.7 copy-done.8
  11.3 0.0 copy-start.9
  11.3 0.7 copy-done.9
  12.0 314.3 %shard_map.158 = (bf16[1,2,32,2048]{3,2,1,0:T(8,128)(2,1)S(1)}, bf16[1,2,32,2048]{3,2,1,0:T(8,128)(2,1)S(1)}) custom-call(bf16[2,32,2048]{2,1,0:T(8,128)(2,1)S(1)} %copy-done.3, bf16[2,32,2048]{2,1,0:T(8,128)(2,1)S(1)} %copy-done.4, bf16[1,2,32,2048]{3,2,1,0:T(8,128)(2,1)S(1)} %copy-done.5, f32[1,2048]{1,0:T(1,128)S(1)} %copy-done.6, ...), custom_call_target="tpu_custom_call" | custom-call | tf_op jit(solution)/shard_map/pallas_call | solution.py:570
  326.3 0.7 copy.21
  327.0 0.7 copy.22
Async XLA Ops:
  2.2 1.4 copy-start
  3.6 1.4 copy-start.1
  5.0 1.4 copy-start.2
  6.4 0.9 copy-start.3
  7.3 0.9 copy-start.4
  8.3 0.9 copy-start.5
  9.2 0.7 copy-start.6
  9.9 0.7 copy-start.7
  10.6 0.7 copy-start.8
  11.3 0.7 copy-start.9

commit v3 on v2

--- a/solution.py
+++ b/solution.py
@@ -10,6 +10,7 @@
 EPSILON = 1e-06
 MESH = pl.DeviceIdType.MESH
 F32 = jnp.float32
+VMEM = 60 * 1024 * 1024
 BF16 = jnp.bfloat16
 ROWS = 16
 NEAR = 4
@@ -45,6 +46,23 @@
 
 def kernel(
     sizes,
+    entering_hbm,
+    cotangent_hbm,
+    saved_hbm,
+    gain_f_hbm,
+    gain_b_hbm,
+    route_f_hbm,
+    route_b_hbm,
+    share_f_hbm,
+    share_b_hbm,
+    gate_f,
+    up_f,
+    down_f,
+    gate_b,
+    up_b,
+    down_b,
+    out_f,
+    out_b,
     entering,
     cotangent,
     saved,
@@ -54,14 +72,6 @@
     route_b,
     share_f,
     share_b,
-    gate_f,
-    up_f,
-    down_f,
-    gate_b,
-    up_b,
-    down_b,
-    out_f,
-    out_b,
     gu_f,
     dn_f,
     gu_b,
@@ -90,6 +100,7 @@
     rsaved,
     kept,
     w_sem,
+    i_sem,
     ein_sem,
     rin_sem,
     sin_sem,
@@ -129,7 +140,25 @@
         (down_b.at[0, 0], dn_b),
     ]
     loads = [pltpu.make_async_copy(s, d, w_sem.at[i]) for i, (s, d) in enumerate(weights)]
-    for load in (loads[3], loads[4], loads[0], loads[1], loads[2], loads[5]):
+    inputs = [
+        pltpu.make_async_copy(s, d, i_sem.at[i])
+        for i, (s, d) in enumerate(
+            [
+                (route_f_hbm, route_f),
+                (route_b_hbm, route_b),
+                (entering_hbm, entering),
+                (cotangent_hbm, cotangent),
+                (share_f_hbm, share_f),
+                (share_b_hbm, share_b),
+                (saved_hbm, saved),
+                (gain_f_hbm, gain_f),
+                (gain_b_hbm, gain_b),
+            ]
+        )
+    ]
+    for load in inputs:
+        load.start()
+    for load in loads:
         load.start()
 
     barrier = pltpu.get_barrier_semaphore()
@@ -174,20 +203,22 @@
         return jnp.sum(jnp.where(eye, row, 0.0), axis=1, keepdims=True)
 
     def code_of(route_column):
-        member = (iota((tokens, 128), 1) == route_column).astype(BF16)
+        member = (iota((tokens, 128), 1).astype(F32) == route_column).astype(BF16)
         same = dot_nt(member, member)
         before = iota((tokens, tokens), 1) < iota((tokens, tokens), 0)
         slot = jnp.sum(jnp.where(before, same, 0.0), axis=1, keepdims=True)
-        return route_column.astype(F32) * ROWS + slot
+        return route_column * ROWS + slot
 
     def expanded(code):
         column = jnp.concatenate([code + q * cap for q in range(parts)], axis=0)
         return (iota((parts * tokens, total), 1).astype(F32) == column).astype(BF16)
 
+    inputs[0].wait()
+    inputs[1].wait()
     codes = []
     for micro_index in range(micro):
         for route in (route_f, route_b):
-            codes.append(code_of(route[0, micro_index]))
+            codes.append(code_of(row_to_column(route[micro_index].astype(F32))))
     def chunk_row(index):
         return lax.rem(index, rows) // cap * ROWS + index // rows * cap + lax.rem(index, cap)
 
@@ -217,7 +248,7 @@
             ).start()
             return carry
 
-        lax.fori_loop(0, count, send, 0)
+        lax.fori_loop(0, count, send, 0, unroll=True)
 
     def send_group(source, target, send_sem, recv_sem):
         send_chunks(source, target, lambda peer: stage, 1, group - 1, send_sem, recv_sem)
@@ -226,24 +257,36 @@
     def wait_bytes(ref, sem):
         pltpu.make_async_copy(ref, ref, sem).wait()
 
-    greeted = (
-        group - 1
-        + group // 2
-        + jnp.where(has_next, group, 0)
-        + jnp.where(first, 0, 1)
-        + jnp.where(at_home, 0, 1)
-    )
-    pl.semaphore_wait(barrier, greeted)
-
-    def deal(micro_index):
+    def place(micro_index):
         for c in (2 * micro_index, 2 * micro_index + 1):
             source = entering if c % 2 == 0 else cotangent
             disp[c] = scatter(expanded(codes[c]), source[micro_index])
+
+    def deal(micro_index):
+        for c in (2 * micro_index, 2 * micro_index + 1):
             send_group(disp.at[c], ein.at[c], disp_sem.at[c], ein_sem.at[c])
 
+    def place_saved(micro_index):
+        sdisp[micro_index] = scatter(
+            expanded(codes[2 * micro_index + 1]), saved[0, micro_index]
+        )
+
+    def deal_saved(micro_index):
+        send_group(
+            sdisp.at[micro_index], sin.at[micro_index], sdisp_sem.at[micro_index], sin_sem.at[micro_index]
+        )
+
+    inputs[6].wait()
+    place_saved(0)
+    inputs[2].wait()
+    inputs[3].wait()
+
     @pl.when(first)
     def _():
-        deal(0)
+        place(0)
+
+    inputs[4].wait()
+    inputs[5].wait()
 
     for direction, share in ((0, share_f), (1, share_b)):
         column = jnp.zeros((rows * micro, 1), F32)
@@ -259,19 +302,28 @@
         msend[:, :, direction * 64 : direction * 64 + 64] = jnp.broadcast_to(
             column, (rows * micro, 64)
         ).reshape(group, cap * micro, 64)
-    send_group(msend, mrecv, msend_sem, m_sem)
-
-    for micro_index in range(micro):
-        sdisp[micro_index] = scatter(expanded(codes[2 * micro_index + 1]), saved[0, micro_index])
-        send_group(
-            sdisp.at[micro_index], sin.at[micro_index], sdisp_sem.at[micro_index], sin_sem.at[micro_index]
-        )
 
     lane = iota((tokens, 128), 1)
     packed = jnp.zeros((tokens, 128), F32)
     for c in range(chains):
         packed = packed + jnp.where(lane == c, codes[c], 0.0)
     csend[...] = packed
+
+    greeted = (
+        group - 1
+        + group // 2
+        + jnp.where(has_next, group, 0)
+        + jnp.where(first, 0, 1)
+        + jnp.where(at_home, 0, 1)
+    )
+    pl.semaphore_wait(barrier, greeted)
+
+    @pl.when(first)
+    def _():
+        deal_saved(0)
+        deal(0)
+
+    send_group(msend, mrecv, msend_sem, m_sem)
 
     def code_copy(target, send_sem, recv_sem, pipe):
         return pltpu.make_async_remote_copy(
@@ -454,6 +506,29 @@
                 device_id_type=MESH,
             ).start()
 
+    def prepare_relay():
+        wait_bytes(crecv, c_sem)
+        for c in range(chains):
+            aexp[c] = expanded(crecv[:, c : c + 1])
+
+        @pl.when(has_next)
+        def _():
+            wait_bytes(cnext, cnext_sem)
+            for c in range(chains):
+                rmat[c] = dot_tn(expanded(cnext[:, c : c + 1]), aexp[c]).astype(BF16)
+
+    @pl.when(first)
+    def _():
+        place_saved(1)
+        deal_saved(1)
+
+    @pl.when(jnp.logical_not(first))
+    def _():
+        prepare_relay()
+        deal_saved(0)
+        place_saved(1)
+        deal_saved(1)
+
     wait_bytes(mrecv, m_sem)
     mflat[...] = mrecv[...].reshape(rows * micro, 128)
     for micro_index in range(micro):
@@ -461,30 +536,28 @@
         for direction in range(2):
             column = lanes[:, direction * 64 : direction * 64 + 1]
             shares[2 * micro_index + direction] = jnp.broadcast_to(column, (rows, 128))
-    loads[3].wait()
-    loads[4].wait()
-    for micro_index in range(micro):
-        prepare_backward(micro_index)
-
-    wait_bytes(crecv, c_sem)
-    for c in range(chains):
-        aexp[c] = expanded(crecv[:, c : c + 1])
-
-    @pl.when(has_next)
-    def _():
-        wait_bytes(cnext, cnext_sem)
-        for c in range(chains):
-            rmat[c] = dot_tn(expanded(cnext[:, c : c + 1]), aexp[c]).astype(BF16)
-
-    for i in (0, 1, 2, 5):
-        loads[i].wait()
+    for load in inputs[7:] + loads:
+        load.wait()
+
+    prepare_backward(0)
+
+    @pl.when(jnp.logical_not(first))
+    def _():
+        prepare_backward(1)
 
     def experts(micro_index):
         expert_forward(micro_index)
-        expert_backward(micro_index)
 
         @pl.when(jnp.logical_and(first, micro_index == 0))
         def _():
+            prepare_backward(1)
+
+        expert_backward(micro_index)
+
+        @pl.when(jnp.logical_and(first, micro_index == 0))
+        def _():
+            prepare_relay()
+            place(1)
             deal(1)
 
     def relays(micro_index):
@@ -572,9 +645,18 @@
                 kernel, (stages, group, micro, tokens, width, hidden_width, cap)
             ),
             out_shape=(state, state),
-            in_specs=[vmem] * 9 + [anywhere] * 6,
+            in_specs=[anywhere] * 15,
             out_specs=(vmem, vmem),
             scratch_shapes=[
+                pltpu.VMEM((micro, tokens, width), BF16),
+                pltpu.VMEM((micro, tokens, width), BF16),
+                pltpu.VMEM((1, micro, tokens, width), BF16),
+                pltpu.VMEM((1, width), F32),
+                pltpu.VMEM((1, width), F32),
+                pltpu.VMEM((micro, 1, tokens), jnp.int32),
+                pltpu.VMEM((micro, 1, tokens), jnp.int32),
+                pltpu.VMEM((1, micro, tokens), F32),
+                pltpu.VMEM((1, micro, tokens), F32),
                 pltpu.VMEM((width, 2 * hidden_width), BF16),
                 pltpu.VMEM((hidden_width, width), BF16),
                 pltpu.VMEM((width, 2 * hidden_width), BF16),
@@ -603,6 +685,7 @@
                 pltpu.VMEM((micro, rows, 128), F32),
                 pltpu.VMEM((chains, tokens, width), BF16),
                 dma((6,)),
+                dma((9,)),
                 dma((chains,)),
                 dma((chains,)),
                 dma((micro,)),
@@ -620,7 +703,7 @@
                 dma((chains,)),
             ],
             compiler_params=pltpu.CompilerParams(
-                collective_id=0, has_side_effects=True, vmem_limit_bytes=48 * 1024 * 1024
+                collective_id=0, has_side_effects=True, vmem_limit_bytes=VMEM
             ),
         )(
             entering,
@@ -628,8 +711,8 @@
             saved_inputs,
             first_gain,
             second_gain,
-            first_route,
-            second_route,
+            first_route.reshape(micro, 1, tokens),
+            second_route.reshape(micro, 1, tokens),
             first_share,
             second_share,
             first_gate,

time: 328 us -> 316 us (0.963)
  local copies, waits for them, and re-layouts: 12.8 us -> 3.34 us
    unnamed x24 -> x2, local copies, waits for them, and re-layouts: 12.8 us -> 3.34 us
where the time goes in v3:
time: 316 us
  Pallas kernels  312 us (99%)
  local copies, waits for them, and re-layouts  3.34 us (1%)
    pallas_call x1, Pallas kernels, local(): pl.pallas_call(functools.partial(kernel, (stages, group, micro, tokens, w...  312 us

profile of v3, /device:TPU:121, one launch (start us, length us, event | category | flops | bytes accessed | tf_op | source)
XLA Modules:
  0.0 316.0 jit_solution(3308048816339205544)
XLA Ops:
  0.6 312.0 %shard_map.158 = (bf16[1,2,32,2048]{3,2,1,0:T(8,128)(2,1)}, bf16[1,2,32,2048]{3,2,1,0:T(8,128)(2,1)}) custom-call(bf16[2,32,2048]{2,1,0:T(8,128)(2,1)} %entering_hbm.1, bf16[2,32,2048]{2,1,0:T(8,128)(2,1)} %cotangent_hbm.1, bf16[1,2,32,2048]{3,2,1,0:T(8,128)(2,1)} %saved_hbm.1, f32[1,2048]{1,0:T(1,128)} %gain_f_hbm.1, f32[1,2048]{1,0:T(1,128)} %gain_b_hbm.1, ...), custom_call_target="tpu_custom_call" | custom-call | tf_op jit(solution)/shard_map/pallas_call | solution.py:643
  312.7 1.7 copy.21
  314.4 1.7 copy.22

commit v4 on v3

--- a/solution.py
+++ b/solution.py
@@ -486,6 +486,8 @@
                 ein_sem.at[c],
             )
 
+    def keep(micro_index, direction):
+        c = 2 * micro_index + direction
         rows_kept = dot(aexp[c], rin[c].reshape(total, wide)).astype(BF16)
         for q in range(parts):
             kept[c, :, q * wide : (q + 1) * wide] = rows_kept[q * tokens : (q + 1) * tokens]
@@ -563,6 +565,8 @@
     def relays(micro_index):
         relay(micro_index, 0)
         relay(micro_index, 1)
+        keep(micro_index, 0)
+        keep(micro_index, 1)
 
     def step(turn, carry):
         odd, late = turn % 2, turn // 2

time: 316 us -> 320 us (1.013)
  Pallas kernels: 312 us -> 316 us
    pallas_call x1, Pallas kernels: 312 us -> 316 us  [local(): pl.pallas_call(functools.partial(kernel, (stages, group, micro, tokens, w...]
where the time goes in v4:
time: 320 us
  Pallas kernels  316 us (99%)
  local copies, waits for them, and re-layouts  3.34 us (1%)
    pallas_call x1, Pallas kernels, local(): pl.pallas_call(functools.partial(kernel, (stages, group, micro, tokens, w...  316 us

profile of v4, /device:TPU:121, one launch (start us, length us, event | category | flops | bytes accessed | tf_op | source)
XLA Modules:
  0.0 320.1 jit_solution(14638805908318095244)
XLA Ops:
  0.6 316.2 %shard_map.158 = (bf16[1,2,32,2048]{3,2,1,0:T(8,128)(2,1)}, bf16[1,2,32,2048]{3,2,1,0:T(8,128)(2,1)}) custom-call(bf16[2,32,2048]{2,1,0:T(8,128)(2,1)} %entering_hbm.1, bf16[2,32,2048]{2,1,0:T(8,128)(2,1)} %cotangent_hbm.1, bf16[1,2,32,2048]{3,2,1,0:T(8,128)(2,1)} %saved_hbm.1, f32[1,2048]{1,0:T(1,128)} %gain_f_hbm.1, f32[1,2048]{1,0:T(1,128)} %gain_b_hbm.1, ...), custom_call_target="tpu_custom_call" | custom-call | tf_op jit(solution)/shard_map/pallas_call | solution.py:647
  316.8 1.7 copy.21
  318.5 1.7 copy.22
